TPU v7x, 128 devices: a whole 4x4x4 slice. The times are simulated.
128 devices in a mesh: src: 8 (over x, z_hi), tgt: 16 (over y, z_lo, core).
Axes of the slice: x: 4, y: 4, z: 4 (z_hi: 2, z_lo: 2; z = z_hi * 2 + z_lo), core: 2. Of those that a mesh axis runs over, the one named last changes fastest.
Arguments:
- noise: bfloat16 [4096, 2048], P(('src', 'tgt')), may hold values from -6 to 6
- data: bfloat16 [4096, 2048], P(('src', 'tgt')), may hold values from -6 to 6
- t_index: int32 [4096], P(('src', 'tgt')), may hold values from 0 to 1000
- embed_weight: bfloat16 [64, 2048], replicated, may hold values from -0.75 to 0.75
- position: bfloat16 [32, 2048], replicated, may hold values from -6 to 6
- norm_gain: float32 [2048], replicated, may hold values from 0.5 to 1.5
- qkv_weight: bfloat16 [2048, 6144], P(None, 'tgt'), may hold values from -0.125 to 0.125
Outputs:
- velocity: bfloat16 [4096, 2048], P(('src', 'tgt'))
- qkv: bfloat16 [131072, 6144], P(('src', 'tgt'))
All inputs are finite; a program needn't handle non-finite values.
Results may differ from a plain program's by a relative error of at most 0.014.
Values may be sent and summed in bfloat16 or wider, within the bound.
No kernel may reach another device: no remote copies, remote signals or barrier semaphores. Data moves between devices by JAX's collectives and lax.ppermute only.
A program may use at most 448 MiB of HBM per device.

v0:
```python
import jax
import jax.numpy as jnp
from jax import lax
from jax.sharding import PartitionSpec as P

ITERS = 3
TGRID = 1000


def joined(value, axis, join):
    pieces = jax.tree.map(lambda part: lax.all_gather(part, axis), value)
    head = jax.tree.map(lambda part: part[0], pieces)
    tail = jax.tree.map(lambda part: part[1:], pieces)
    total, _ = lax.scan(lambda total, share: (join(total, share), None), head, tail)
    return total


def combine_lse(first, second):
    highest = jnp.maximum(first[0], second[0])
    return (
        highest,
        first[1] * jnp.exp(first[0] - highest) + second[1] * jnp.exp(second[0] - highest),
    )


def row_potential(scores, epsilon):
    local_peak = jnp.max(scores, axis=1)
    local_total = jnp.sum(jnp.exp(scores - local_peak[:, None]), axis=1)
    peak_all, total_all = joined((local_peak, local_total), "tgt", combine_lse)
    return -epsilon * (peak_all + jnp.log(total_all))


def col_potential(scores, epsilon):
    local_peak = jnp.max(scores, axis=0)
    local_total = jnp.sum(jnp.exp(scores - local_peak[None, :]), axis=0)
    peak_all, total_all = joined((local_peak, local_total), "src", combine_lse)
    return -epsilon * (peak_all + jnp.log(total_all))


def embed_rows(samples, embed_weight, position, norm_gain):
    count = samples.shape[0]
    patch_count = position.shape[0]
    patch_in = embed_weight.shape[0]
    width = embed_weight.shape[1]
    patches = samples.reshape(count * patch_count, patch_in)
    embedded = jnp.dot(patches, embed_weight, preferred_element_type=jnp.float32).reshape(
        count, patch_count, width
    )
    embedded = embedded + position.astype(jnp.float32)[None]
    meansq = jnp.mean(embedded * embedded, axis=-1, keepdims=True)
    normed = (embedded * lax.rsqrt(meansq + 1e-06) * norm_gain).astype(jnp.bfloat16)
    return normed.reshape(count * patch_count, width)


def local(noise, data, t_index, embed_weight, position, norm_gain, qkv_weight):
    latent = noise.shape[1]
    own_rows = noise.shape[0]
    noise_block = lax.all_gather(noise, "tgt", axis=0, tiled=True)
    data_block = lax.all_gather(data, "src", axis=0, tiled=True)
    noise_sq = jnp.sum(jnp.square(noise_block.astype(jnp.float32)), axis=1)
    data_sq = jnp.sum(jnp.square(data_block.astype(jnp.float32)), axis=1)
    cross_term = lax.dot_general(
        noise_block, data_block, (((1,), (1,)), ((), ())), preferred_element_type=jnp.float32
    )
    cost = (noise_sq[:, None] + data_sq[None, :] - 2.0 * cross_term) / latent
    col_pot = jnp.zeros((data_block.shape[0],), jnp.float32)
    row_pot = jnp.zeros((noise_block.shape[0],), jnp.float32)
    epsilon = 0.04
    for step in range(ITERS):
        epsilon = 0.04 * 0.45**step
        row_pot = row_potential((col_pot[None, :] - cost) / epsilon, epsilon)
        col_pot = col_potential((row_pot[:, None] - cost) / epsilon, epsilon)
    scores = (col_pot[None, :] - cost) / epsilon
    offset = lax.axis_index("tgt") * own_rows
    local_peak = jnp.max(scores, axis=1)
    local_total = jnp.sum(jnp.exp(scores - local_peak[:, None]), axis=1)
    peak_all, denom = joined((local_peak, local_total), "tgt", combine_lse)
    coupling = jnp.exp(scores - peak_all[:, None]).astype(jnp.bfloat16)
    partial_sum = jnp.dot(coupling, data_block, preferred_element_type=jnp.float32)
    numer = lax.psum_scatter(
        partial_sum.astype(jnp.bfloat16), "tgt", scatter_dimension=0, tiled=True
    ).astype(jnp.float32)
    own_denom = lax.dynamic_slice_in_dim(denom, offset, own_rows, 0)
    target = numer / own_denom[:, None]
    noise_own = noise.astype(jnp.float32)
    velocity = (target - noise_own).astype(jnp.bfloat16)
    times = t_index.astype(jnp.float32) / TGRID
    mixed = ((1.0 - times)[:, None] * noise_own + times[:, None] * target).astype(jnp.bfloat16)
    normed = embed_rows(mixed, embed_weight, position, norm_gain)
    qkv = jnp.dot(
        normed,
        lax.all_gather(qkv_weight, "tgt", axis=1, tiled=True),
        preferred_element_type=jnp.float32,
    ).astype(jnp.bfloat16)
    return (velocity, qkv)


def solution(mesh):
    return jax.shard_map(
        local,
        mesh=mesh,
        in_specs=(
            P(("src", "tgt"), None),
            P(("src", "tgt"), None),
            P(("src", "tgt")),
            P(),
            P(),
            P(),
            P(None, "tgt"),
        ),
        out_specs=(P(("src", "tgt"), None), P(("src", "tgt"), None)),
        check_vma=False,
    )
```

profile of v0, /device:TPU:1, one launch (start us, length us, event | category | flops | bytes accessed | tf_op | source)
XLA Modules:
  0.0 597.8 jit_solution(4102030687520857336)
XLA Ops:
  7.2 0.7 all-gather.34.cloned.1.call-update
  8.0 0.7 all-gather.32.cloned.1.call-update
  8.7 51.4 %all-gather.34.cloned.1.call-done = bf16[256,2048]{1,0:T(8,128)(2,1)} async-done(((bf16[32,2048]{1,0:T(8,128)(2,1)}), bf16[256,2048]{1,0:T(8,128)(2,1)}) %all-gather.34.cloned.1.call-update) | async-done | bytes 1048592 | tf_op jit(solution)/shard_map/all_gather | solution.py:59
  60.1 1.5 multiply_reduce_fusion.2
  61.6 34.1 %all-gather.32.cloned.1.call-done = bf16[512,2048]{1,0:T(8,128)(2,1)} async-done(((bf16[32,2048]{1,0:T(8,128)(2,1)}), bf16[512,2048]{1,0:T(8,128)(2,1)}) %all-gather.32.cloned.1.call-update) | async-done | bytes 2097168 | tf_op jit(solution)/shard_map/all_gather | solution.py:58
  95.7 2.1 multiply_reduce_fusion.1
  97.7 2.7 fusion.2
  100.5 0.1 exponential_reduce_fusion.6
  100.6 18.1 %all-gather.15 = f32[16,1,512]{2,1,0:T(1,128)S(1)} all-gather(f32[1,1,512]{2,1,0:T(1,128)S(1)} %bitcast.176), channel_id=3, replica_groups=mesh['src'=8,'tgt'=16] {'tgt'}, dimensions={0}, use_global_device_ids=true | all-gather | bytes 34816 | tf_op jit(solution)/shard_map/all_gather | solution.py:11
  118.8 16.3 %all-gather.14 = f32[16,1,512]{2,1,0:T(1,128)S(1)} all-gather(f32[1,1,512]{2,1,0:T(1,128)S(1)} %bitcast.173), channel_id=2, replica_groups=mesh['src'=8,'tgt'=16] {'tgt'}, dimensions={0}, use_global_device_ids=true | all-gather | bytes 34816 | tf_op jit(solution)/shard_map/all_gather | solution.py:11
  135.1 0.8 while.84
  136.1 0.2 exponential_reduce_fusion.5
  136.3 19.5 %all-gather.16 = f32[8,1,256]{2,1,0:T(1,128)S(1)} all-gather(f32[1,1,256]{2,1,0:T(1,128)S(1)} %bitcast.170), channel_id=4, replica_groups=mesh['src'=8,'tgt'=16] {'src'}, dimensions={0}, use_global_device_ids=true | all-gather | bytes 9216 | tf_op jit(solution)/shard_map/all_gather | solution.py:11
  155.8 14.6 %all-gather.17 = f32[8,1,256]{2,1,0:T(1,128)S(1)} all-gather(f32[1,1,256]{2,1,0:T(1,128)S(1)} %bitcast.178), channel_id=5, replica_groups=mesh['src'=8,'tgt'=16] {'src'}, dimensions={0}, use_global_device_ids=true | all-gather | bytes 9216 | tf_op jit(solution)/shard_map/all_gather | solution.py:11
  170.4 0.3 while.85
  170.8 0.1 fusion.4
  170.9 0.2 exponential_reduce_fusion.4
  171.1 24.3 %all-gather.19 = f32[16,1,512]{2,1,0:T(1,128)S(1)} all-gather(f32[1,1,512]{2,1,0:T(1,128)S(1)} %bitcast.174), channel_id=7, replica_groups=mesh['src'=8,'tgt'=16] {'tgt'}, dimensions={0}, use_global_device_ids=true | all-gather | bytes 34816 | tf_op jit(solution)/shard_map/all_gather | solution.py:11
  195.5 16.9 %all-gather.18 = f32[16,1,512]{2,1,0:T(1,128)S(1)} all-gather(f32[1,1,512]{2,1,0:T(1,128)S(1)} %bitcast.167), channel_id=6, replica_groups=mesh['src'=8,'tgt'=16] {'tgt'}, dimensions={0}, use_global_device_ids=true | all-gather | bytes 34816 | tf_op jit(solution)/shard_map/all_gather | solution.py:11
  212.4 0.8 while.86
  213.4 0.2 exponential_reduce_fusion.3
  213.6 17.9 %all-gather.20 = f32[8,1,256]{2,1,0:T(1,128)S(1)} all-gather(f32[1,1,256]{2,1,0:T(1,128)S(1)} %bitcast.171), channel_id=8, replica_groups=mesh['src'=8,'tgt'=16] {'src'}, dimensions={0}, use_global_device_ids=true | all-gather | bytes 9216 | tf_op jit(solution)/shard_map/all_gather | solution.py:11
  231.4 14.6 %all-gather.21 = f32[8,1,256]{2,1,0:T(1,128)S(1)} all-gather(f32[1,1,256]{2,1,0:T(1,128)S(1)} %bitcast.179), channel_id=9, replica_groups=mesh['src'=8,'tgt'=16] {'src'}, dimensions={0}, use_global_device_ids=true | all-gather | bytes 9216 | tf_op jit(solution)/shard_map/all_gather | solution.py:11
  246.1 0.3 while.87
  246.4 0.1 fusion.6
  246.6 0.2 exponential_reduce_fusion.2
  246.8 24.3 %all-gather.23 = f32[16,1,512]{2,1,0:T(1,128)S(1)} all-gather(f32[1,1,512]{2,1,0:T(1,128)S(1)} %bitcast.175), channel_id=11, replica_groups=mesh['src'=8,'tgt'=16] {'tgt'}, dimensions={0}, use_global_device_ids=true | all-gather | bytes 34816 | tf_op jit(solution)/shard_map/all_gather | solution.py:11
  271.1 16.9 %all-gather.22 = f32[16,1,512]{2,1,0:T(1,128)S(1)} all-gather(f32[1,1,512]{2,1,0:T(1,128)S(1)} %bitcast.168), channel_id=10, replica_groups=mesh['src'=8,'tgt'=16] {'tgt'}, dimensions={0}, use_global_device_ids=true | all-gather | bytes 34816 | tf_op jit(solution)/shard_map/all_gather | solution.py:11
  288.0 0.8 while.88
  289.0 0.2 exponential_reduce_fusion.1
  289.2 17.9 %all-gather.24 = f32[8,1,256]{2,1,0:T(1,128)S(1)} all-gather(f32[1,1,256]{2,1,0:T(1,128)S(1)} %bitcast.172), channel_id=12, replica_groups=mesh['src'=8,'tgt'=16] {'src'}, dimensions={0}, use_global_device_ids=true | all-gather | bytes 9216 | tf_op jit(solution)/shard_map/all_gather | solution.py:11
  307.1 14.6 %all-gather.25 = f32[8,1,256]{2,1,0:T(1,128)S(1)} all-gather(f32[1,1,256]{2,1,0:T(1,128)S(1)} %bitcast.180), channel_id=13, replica_groups=mesh['src'=8,'tgt'=16] {'src'}, dimensions={0}, use_global_device_ids=true | all-gather | bytes 9216 | tf_op jit(solution)/shard_map/all_gather | solution.py:11
  321.7 0.3 while.89
  322.1 0.1 fusion.8
  322.2 0.2 exponential_reduce_fusion
  322.4 24.3 %all-gather.27 = f32[16,1,512]{2,1,0:T(1,128)S(1)} all-gather(f32[1,1,512]{2,1,0:T(1,128)S(1)} %bitcast.177), channel_id=15, replica_groups=mesh['src'=8,'tgt'=16] {'tgt'}, dimensions={0}, use_global_device_ids=true | all-gather | bytes 34816 | tf_op jit(solution)/shard_map/all_gather | solution.py:11
  346.7 16.9 %all-gather.26 = f32[16,1,512]{2,1,0:T(1,128)S(1)} all-gather(f32[1,1,512]{2,1,0:T(1,128)S(1)} %bitcast.169), channel_id=14, replica_groups=mesh['src'=8,'tgt'=16] {'tgt'}, dimensions={0}, use_global_device_ids=true | all-gather | bytes 34816 | tf_op jit(solution)/shard_map/all_gather | solution.py:11
  363.7 0.8 while.90
  364.5 2.2 convolution_convert_fusion.1
  366.7 0.2 all-gather.36.cloned.1.call-start
  367.0 0.3 all-gather.36.cloned.1.call-update
  367.5 56.1 %reduce-scatter.2.cloned.1.call-done = bf16[32,2048]{1,0:T(8,128)(2,1)} async-done(((bf16[512,2048]{1,0:T(8,128)(2,1)}), bf16[32,2048]{1,0:T(8,128)(2,1)}) %reduce-scatter.2.cloned.1.call-update) | async-done | bytes 131088 | tf_op jit(solution)/shard_map/reduce_scatter | solution.py:80
  423.6 1.7 fusion.11
  425.3 0.2 dot_general.16
  425.6 1.3 multiply_reduce_fusion
  426.9 3.0 multiply_convert_fusion
  430.0 129.0 %all-gather.36.cloned.1.call-done = bf16[2048,6144]{1,0:T(8,128)(2,1)} async-done(((bf16[2048,384]{1,0:T(8,128)(2,1)}), bf16[2048,6144]{1,0:T(8,128)(2,1)}) %all-gather.36.cloned.1.call-update) | async-done | bytes 25165840 | tf_op jit(solution)/shard_map/all_gather | solution.py:92
  558.9 32.3 %convolution_convert_fusion = bf16[1024,6144]{1,0:T(8,128)(2,1)} fusion(bf16[1024,2048]{1,0:T(8,128)(2,1)} %bitcast.124, bf16[2048,6144]{1,0:T(8,128)(2,1)} %all-gather.36.cloned.1.call-done), kind=kOutput, calls=%fused_computation.21 | convolution fusion | flops 25776095232 | bytes 41943040 | tf_op jit(solution)/shard_map/dot_general | solution.py:90
  (233 shorter events, 3.4 us)
Async XLA Ops:
  7.2 418.4 %copy-start = (bf16[64,2048]{1,0:T(8,128)(2,1)S(1)}, bf16[64,2048]{1,0:T(8,128)(2,1)}, u32[]{:S(2)}) copy-start(bf16[64,2048]{1,0:T(8,128)(2,1)} %param.24) | copy-start | bytes 786436
  7.2 52.9 %all-gather.34.cloned.1.call-start = ((), (), s32[]{:S(2)}) async-start(), calls=%async_computation.2 | async-start | bytes 1179648 | tf_op jit(solution)/shard_map/all_gather | solution.py:59
  7.9 87.7 %all-gather.32.cloned.1.call-start = ((), (), s32[]{:S(2)}) async-start(), calls=%async_computation.1 | async-start | bytes 2228224 | tf_op jit(solution)/shard_map/all_gather | solution.py:58
  8.7 414.9 %reduce-scatter.2.cloned.1.call-start = ((), (), s32[]{:S(2)}) async-start(), calls=%async_computation.3 | async-start | bytes 2228224 | tf_op jit(solution)/shard_map/reduce_scatter | solution.py:80
  97.7 266.8 %copy-start.1 = (bf16[256,2048]{1,0:T(8,128)(2,1)S(1)}, bf16[256,2048]{1,0:T(8,128)(2,1)}, u32[]{:S(2)}) copy-start(bf16[256,2048]{1,0:T(8,128)(2,1)} %all-gather.34.cloned.1.call-done) | copy-start | bytes 3145732
  135.9 231.4 %copy-start.3 = (bf16[32,2048]{1,0:T(8,128)(2,1)S(1)}, bf16[32,2048]{1,0:T(8,128)(2,1)}, u32[]{:S(2)}) copy-start(bf16[32,2048]{1,0:T(8,128)(2,1)} %param.25) | copy-start | bytes 393220
  135.9 231.4 %copy-start.5 = (s32[32]{0:T(128)S(1)}, s32[32]{0:T(128)}, u32[]{:S(2)}) copy-start(s32[32]{0:T(128)} %param.23) | copy-start | bytes 388
  135.9 287.7 %copy-start.2 = (bf16[32,2048]{1,0:T(8,128)(2,1)S(1)}, bf16[32,2048]{1,0:T(8,128)(2,1)}, u32[]{:S(2)}) copy-start(bf16[32,2048]{1,0:T(8,128)(2,1)} %param.21) | copy-start | bytes 393220
  364.5 62.4 %copy-start.4 = (f32[2048]{0:T(1024)S(1)}, f32[2048]{0:T(1024)}, u32[]{:S(2)}) copy-start(f32[2048]{0:T(1024)} %param.26) | copy-start | bytes 24580
  366.7 192.2 %all-gather.36.cloned.1.call-start = ((), (), s32[]{:S(2)}) async-start(), calls=%async_computation.4 | async-start | bytes 26738688 | tf_op jit(solution)/shard_map/all_gather | solution.py:92
Sparse Core Ops, SparseCore 0:
  10.4 49.6 all-gather.33
  61.8 33.8 all-gather.31
  366.9 56.7 reduce-scatter.1
  425.1 133.7 all-gather.35
where the time goes:
time: 598 us
  waiting for transfers between devices  272 us (45%)
  blocking collectives  257 us (43%)
  matrix products  38.6 us (6%)
  between operations  14.1 us (2%)
  other arithmetic  12.3 us (2%)
    all_gather x14, blocking collectives, joined(): pieces = jax.tree.map(lambda part: lax.all_gather(part, axis), value)  257 us
    all_gather x1, waiting for transfers between devices, local(): lax.all_gather(qkv_weight, 'tgt', axis=1, tiled=True)  129 us
    reduce_scatter x1, waiting for transfers between devices, local(): lax.psum_scatter(partial_sum.astype(jnp.bfloat16), 'tgt', scatter_dimensi...  56.1 us
    all_gather x1, waiting for transfers between devices, local(): data_block = lax.all_gather(data, 'src', axis=0, tiled=True)  51.4 us
    all_gather x1, waiting for transfers between devices, local(): noise_block = lax.all_gather(noise, 'tgt', axis=0, tiled=True)  34.1 us
    dot_general x1, matrix products, local(): jnp.dot(normed, lax.all_gather(qkv_weight, 'tgt', axis=1, tiled=True), pr...  32.3 us
  transfers between devices with their start and end apart: 4, of which 4 were waited for; matrix products, arithmetic and copies ran while one was open for 1% of the time, Pallas kernels for 0%

commit v1 on v0

--- a/solution.py
+++ b/solution.py
@@ -56,7 +56,9 @@
     latent = noise.shape[1]
     own_rows = noise.shape[0]
     noise_block = lax.all_gather(noise, "tgt", axis=0, tiled=True)
-    data_block = lax.all_gather(data, "src", axis=0, tiled=True)
+    data_block = jnp.concatenate(
+        lax.all_to_all(jnp.stack([data] * lax.axis_size("src")), "src", 0, 0), axis=0
+    )
     noise_sq = jnp.sum(jnp.square(noise_block.astype(jnp.float32)), axis=1)
     data_sq = jnp.sum(jnp.square(data_block.astype(jnp.float32)), axis=1)
     cross_term = lax.dot_general(

time: 598 us -> 557 us (0.931)
  waiting for transfers between devices: 272 us -> 221 us
  starting transfers between devices: 0.34 us -> 8.46 us
    all_gather x1 -> x0, waiting for transfers between devices: 51.4 us -> none  [local(): data_block = lax.all_gather(data, 'src', axis=0, tiled=True)]
    all_to_all x0 -> x1, waiting for transfers between devices: none -> 15.5 us  [local(): lax.all_to_all(jnp.stack([data] * lax.axis_size('src')), 'src', 0, 0)]
    all_gather x1, waiting for transfers between devices: 34.1 us -> 18.9 us  [local(): noise_block = lax.all_gather(noise, 'tgt', axis=0, tiled=True)]
    all_to_all x0 -> x1, starting transfers between devices: none -> 8.16 us  [local(): lax.all_to_all(jnp.stack([data] * lax.axis_size('src')), 'src', 0, 0)]
  transfers between devices with their start and end apart: 4 -> 4, of which waited for: 4 -> 4; matrix products, arithmetic and copies ran while one was open for 1% -> 2% of each run, Pallas kernels for 0% -> 0%
where the time goes in v1:
time: 557 us; the launch traced here: 556 us
  blocking collectives  259 us (46%)
  waiting for transfers between devices  221 us (40%)
  matrix products  38.2 us (7%)
  between operations  14 us (3%)
  other arithmetic  11 us (2%)
  starting transfers between devices  8.46 us (2%)
    all_gather x14, blocking collectives, joined(): pieces = jax.tree.map(lambda part: lax.all_gather(part, axis), value)  259 us
    all_gather x1, waiting for transfers between devices, local(): lax.all_gather(qkv_weight, 'tgt', axis=1, tiled=True)  129 us
    reduce_scatter x1, waiting for transfers between devices, local(): lax.psum_scatter(partial_sum.astype(jnp.bfloat16), 'tgt', scatter_dimensi...  56.1 us
    dot_general x1, matrix products, local(): jnp.dot(normed, lax.all_gather(qkv_weight, 'tgt', axis=1, tiled=True), pr...  32.3 us
    all_gather x1, waiting for transfers between devices, local(): noise_block = lax.all_gather(noise, 'tgt', axis=0, tiled=True)  18.9 us
    all_to_all x1, waiting for transfers between devices, local(): lax.all_to_all(jnp.stack([data] * lax.axis_size('src')), 'src', 0, 0)  15.5 us
  transfers between devices with their start and end apart: 4, of which 4 were waited for; matrix products, arithmetic and copies ran while one was open for 2% of the time, Pallas kernels for 0%

profile of v1, /device:TPU:1, one launch (start us, length us, event | category | flops | bytes accessed | tf_op | source)
XLA Modules:
  0.0 556.5 jit_solution(14260734142323233431)
XLA Ops:
  7.2 0.7 all-gather.31.cloned.1.call-update
  7.9 2.0 stack.2
  9.9 8.2 %all-to-all-start = ((bf16[8,32,2048]{2,1,0:T(8,128)(2,1)}), bf16[8,32,2048]{2,1,0:T(8,128)(2,1)S(1)}, u32[]{:S(2)}, u32[]{:S(2)}) async-start(bf16[8,32,2048]{2,1,0:T(8,128)(2,1)} %stack.2), calls=%async_computation | async-start | bytes 2097152 | tf_op jit(solution)/shard_map/all_to_all | solution.py:60
  18.1 15.5 %all-to-all-done = bf16[8,32,2048]{2,1,0:T(8,128)(2,1)S(1)} async-done(((bf16[8,32,2048]{2,1,0:T(8,128)(2,1)}), bf16[8,32,2048]{2,1,0:T(8,128)(2,1)S(1)}, u32[]{:S(2)}, u32[]{:S(2)}) %all-to-all-start) | async-done | bytes 1048608 | tf_op jit(solution)/shard_map/all_to_all | solution.py:60
  33.6 0.3 multiply_reduce_fusion.2
  34.0 18.9 %all-gather.31.cloned.1.call-done = bf16[512,2048]{1,0:T(8,128)(2,1)} async-done(((bf16[32,2048]{1,0:T(8,128)(2,1)}), bf16[512,2048]{1,0:T(8,128)(2,1)}) %all-gather.31.cloned.1.call-update) | async-done | bytes 2097168 | tf_op jit(solution)/shard_map/all_gather | solution.py:58
  52.8 2.1 multiply_reduce_fusion.1
  54.9 2.4 fusion.2
  57.3 0.1 exponential_reduce_fusion.6
  57.4 18.1 %all-gather.15 = f32[16,1,512]{2,1,0:T(1,128)S(1)} all-gather(f32[1,1,512]{2,1,0:T(1,128)S(1)} %bitcast.179), channel_id=3, replica_groups=mesh['src'=8,'tgt'=16] {'tgt'}, dimensions={0}, use_global_device_ids=true | all-gather | bytes 34816 | tf_op jit(solution)/shard_map/all_gather | solution.py:11
  75.6 16.3 %all-gather.14 = f32[16,1,512]{2,1,0:T(1,128)S(1)} all-gather(f32[1,1,512]{2,1,0:T(1,128)S(1)} %bitcast.176), channel_id=2, replica_groups=mesh['src'=8,'tgt'=16] {'tgt'}, dimensions={0}, use_global_device_ids=true | all-gather | bytes 34816 | tf_op jit(solution)/shard_map/all_gather | solution.py:11
  91.9 0.8 while.84
  92.9 0.2 exponential_reduce_fusion.5
  93.1 21.4 %all-gather.16 = f32[8,1,256]{2,1,0:T(1,128)S(1)} all-gather(f32[1,1,256]{2,1,0:T(1,128)S(1)} %bitcast.173), channel_id=4, replica_groups=mesh['src'=8,'tgt'=16] {'src'}, dimensions={0}, use_global_device_ids=true | all-gather | bytes 9216 | tf_op jit(solution)/shard_map/all_gather | solution.py:11
  114.5 14.6 %all-gather.17 = f32[8,1,256]{2,1,0:T(1,128)S(1)} all-gather(f32[1,1,256]{2,1,0:T(1,128)S(1)} %bitcast.181), channel_id=5, replica_groups=mesh['src'=8,'tgt'=16] {'src'}, dimensions={0}, use_global_device_ids=true | all-gather | bytes 9216 | tf_op jit(solution)/shard_map/all_gather | solution.py:11
  129.1 0.3 while.85
  129.6 0.2 exponential_reduce_fusion.4
  129.8 24.3 %all-gather.19 = f32[16,1,512]{2,1,0:T(1,128)S(1)} all-gather(f32[1,1,512]{2,1,0:T(1,128)S(1)} %bitcast.177), channel_id=7, replica_groups=mesh['src'=8,'tgt'=16] {'tgt'}, dimensions={0}, use_global_device_ids=true | all-gather | bytes 34816 | tf_op jit(solution)/shard_map/all_gather | solution.py:11
  154.1 16.9 %all-gather.18 = f32[16,1,512]{2,1,0:T(1,128)S(1)} all-gather(f32[1,1,512]{2,1,0:T(1,128)S(1)} %bitcast.170), channel_id=6, replica_groups=mesh['src'=8,'tgt'=16] {'tgt'}, dimensions={0}, use_global_device_ids=true | all-gather | bytes 34816 | tf_op jit(solution)/shard_map/all_gather | solution.py:11
  171.1 0.8 while.86
  172.1 0.2 exponential_reduce_fusion.3
  172.3 17.9 %all-gather.20 = f32[8,1,256]{2,1,0:T(1,128)S(1)} all-gather(f32[1,1,256]{2,1,0:T(1,128)S(1)} %bitcast.174), channel_id=8, replica_groups=mesh['src'=8,'tgt'=16] {'src'}, dimensions={0}, use_global_device_ids=true | all-gather | bytes 9216 | tf_op jit(solution)/shard_map/all_gather | solution.py:11
  190.1 14.6 %all-gather.21 = f32[8,1,256]{2,1,0:T(1,128)S(1)} all-gather(f32[1,1,256]{2,1,0:T(1,128)S(1)} %bitcast.182), channel_id=9, replica_groups=mesh['src'=8,'tgt'=16] {'src'}, dimensions={0}, use_global_device_ids=true | all-gather | bytes 9216 | tf_op jit(solution)/shard_map/all_gather | solution.py:11
  204.8 0.3 while.87
  205.1 0.1 fusion.6
  205.3 0.2 exponential_reduce_fusion.2
  205.5 24.3 %all-gather.23 = f32[16,1,512]{2,1,0:T(1,128)S(1)} all-gather(f32[1,1,512]{2,1,0:T(1,128)S(1)} %bitcast.178), channel_id=11, replica_groups=mesh['src'=8,'tgt'=16] {'tgt'}, dimensions={0}, use_global_device_ids=true | all-gather | bytes 34816 | tf_op jit(solution)/shard_map/all_gather | solution.py:11
  229.8 16.9 %all-gather.22 = f32[16,1,512]{2,1,0:T(1,128)S(1)} all-gather(f32[1,1,512]{2,1,0:T(1,128)S(1)} %bitcast.171), channel_id=10, replica_groups=mesh['src'=8,'tgt'=16] {'tgt'}, dimensions={0}, use_global_device_ids=true | all-gather | bytes 34816 | tf_op jit(solution)/shard_map/all_gather | solution.py:11
  246.7 0.8 while.88
  247.7 0.2 exponential_reduce_fusion.1
  247.9 17.9 %all-gather.24 = f32[8,1,256]{2,1,0:T(1,128)S(1)} all-gather(f32[1,1,256]{2,1,0:T(1,128)S(1)} %bitcast.175), channel_id=12, replica_groups=mesh['src'=8,'tgt'=16] {'src'}, dimensions={0}, use_global_device_ids=true | all-gather | bytes 9216 | tf_op jit(solution)/shard_map/all_gather | solution.py:11
  265.8 14.6 %all-gather.25 = f32[8,1,256]{2,1,0:T(1,128)S(1)} all-gather(f32[1,1,256]{2,1,0:T(1,128)S(1)} %bitcast.183), channel_id=13, replica_groups=mesh['src'=8,'tgt'=16] {'src'}, dimensions={0}, use_global_device_ids=true | all-gather | bytes 9216 | tf_op jit(solution)/shard_map/all_gather | solution.py:11
  280.4 0.3 while.89
  280.8 0.1 fusion.8
  280.9 0.2 exponential_reduce_fusion
  281.1 24.3 %all-gather.27 = f32[16,1,512]{2,1,0:T(1,128)S(1)} all-gather(f32[1,1,512]{2,1,0:T(1,128)S(1)} %bitcast.180), channel_id=15, replica_groups=mesh['src'=8,'tgt'=16] {'tgt'}, dimensions={0}, use_global_device_ids=true | all-gather | bytes 34816 | tf_op jit(solution)/shard_map/all_gather | solution.py:11
  305.4 16.9 %all-gather.26 = f32[16,1,512]{2,1,0:T(1,128)S(1)} all-gather(f32[1,1,512]{2,1,0:T(1,128)S(1)} %bitcast.172), channel_id=14, replica_groups=mesh['src'=8,'tgt'=16] {'tgt'}, dimensions={0}, use_global_device_ids=true | all-gather | bytes 34816 | tf_op jit(solution)/shard_map/all_gather | solution.py:11
  322.4 0.8 while.90
  323.2 2.2 convolution_convert_fusion.1
  325.4 0.2 all-gather.33.cloned.1.call-start
  325.7 0.5 all-gather.33.cloned.1.call-update
  326.3 56.1 %reduce-scatter.2.cloned.1.call-done = bf16[32,2048]{1,0:T(8,128)(2,1)} async-done(((bf16[512,2048]{1,0:T(8,128)(2,1)}), bf16[32,2048]{1,0:T(8,128)(2,1)}) %reduce-scatter.2.cloned.1.call-update) | async-done | bytes 131088 | tf_op jit(solution)/shard_map/reduce_scatter | solution.py:82
  382.4 1.7 fusion.11
  384.1 0.2 dot_general.16
  384.3 1.3 multiply_reduce_fusion
  385.7 3.0 multiply_convert_fusion
  388.7 128.9 %all-gather.33.cloned.1.call-done = bf16[2048,6144]{1,0:T(8,128)(2,1)} async-done(((bf16[2048,384]{1,0:T(8,128)(2,1)}), bf16[2048,6144]{1,0:T(8,128)(2,1)}) %all-gather.33.cloned.1.call-update) | async-done | bytes 25165840 | tf_op jit(solution)/shard_map/all_gather | solution.py:94
  517.6 32.3 %convolution_convert_fusion = bf16[1024,6144]{1,0:T(8,128)(2,1)} fusion(bf16[1024,2048]{1,0:T(8,128)(2,1)} %bitcast.127, bf16[2048,6144]{1,0:T(8,128)(2,1)} %all-gather.33.cloned.1.call-done), kind=kOutput, calls=%fused_computation.21 | convolution fusion | flops 25776095232 | bytes 41943040 | tf_op jit(solution)/shard_map/dot_general | solution.py:92
  (232 shorter events, 3.5 us)
Async XLA Ops:
  7.2 377.2 %copy-start = (bf16[64,2048]{1,0:T(8,128)(2,1)S(1)}, bf16[64,2048]{1,0:T(8,128)(2,1)}, u32[]{:S(2)}) copy-start(bf16[64,2048]{1,0:T(8,128)(2,1)} %param.24) | copy-start | bytes 786436
  7.2 45.7 %all-gather.31.cloned.1.call-start = ((), (), s32[]{:S(2)}) async-start(), calls=%async_computation.2 | async-start | bytes 2228224 | tf_op jit(solution)/shard_map/all_gather | solution.py:58
  9.9 23.7 %all-to-all-start = ((bf16[8,32,2048]{2,1,0:T(8,128)(2,1)}), bf16[8,32,2048]{2,1,0:T(8,128)(2,1)S(1)}, u32[]{:S(2)}, u32[]{:S(2)}) async-start(bf16[8,32,2048]{2,1,0:T(8,128)(2,1)} %stack.2), calls=%async_computation | async-start | bytes 2097152 | tf_op jit(solution)/shard_map/all_to_all | solution.py:60
  18.1 364.3 %reduce-scatter.2.cloned.1.call-start = ((), (), s32[]{:S(2)}) async-start(), calls=%async_computation.3 | async-start | bytes 2228224 | tf_op jit(solution)/shard_map/reduce_scatter | solution.py:82
  92.7 233.4 %copy-start.2 = (bf16[32,2048]{1,0:T(8,128)(2,1)S(1)}, bf16[32,2048]{1,0:T(8,128)(2,1)}, u32[]{:S(2)}) copy-start(bf16[32,2048]{1,0:T(8,128)(2,1)} %param.25) | copy-start | bytes 393220
  92.7 233.5 %copy-start.4 = (s32[32]{0:T(128)S(1)}, s32[32]{0:T(128)}, u32[]{:S(2)}) copy-start(s32[32]{0:T(128)} %param.23) | copy-start | bytes 388
  92.8 289.6 %copy-start.1 = (bf16[32,2048]{1,0:T(8,128)(2,1)S(1)}, bf16[32,2048]{1,0:T(8,128)(2,1)}, u32[]{:S(2)}) copy-start(bf16[32,2048]{1,0:T(8,128)(2,1)} %param.21) | copy-start | bytes 393220
  323.2 62.5 %copy-start.3 = (f32[2048]{0:T(1024)S(1)}, f32[2048]{0:T(1024)}, u32[]{:S(2)}) copy-start(f32[2048]{0:T(1024)} %param.26) | copy-start | bytes 24580
  325.4 192.2 %all-gather.33.cloned.1.call-start = ((), (), s32[]{:S(2)}) async-start(), calls=%async_computation.4 | async-start | bytes 26738688 | tf_op jit(solution)/shard_map/all_gather | solution.py:94
Sparse Core Ops, SparseCore 0:
  9.7 43.0 all-gather.30
  325.5 56.7 reduce-scatter.1
  384.1 133.5 all-gather.32
